TPU v7x, 512 devices: a whole 4x8x8 slice. The times are simulated.
512 devices in a mesh: mode: 32 (over x, y), orb: 16 (over z, core).
Axes of the slice: x: 4, y: 8, z: 8, core: 2. Of those that a mesh axis runs over, the one named last changes fastest.
Arguments:
- correlators: float32 [512, 2, 256, 256], P('mode', None, 'orb'), may hold values from -6 to 6
- density: float32 [2, 256, 256], P(None, 'orb'), may hold values from -6 to 6
- bare_hamiltonian: float32 [2, 256, 256], P(None, 'orb'), may hold values from -0.375 to 0.375
- coupling: float32 [512], P('mode'), may hold values from -0.25 to 0.25
- propagator: float32 [512, 512], P('mode'), may hold values from -0.25 to 0.25
Outputs:
- correlators_out: float32 [512, 2, 256, 256], P('mode', None, 'orb')
- density_out: float32 [2, 256, 256], P(None, 'orb')
All inputs are finite; a program needn't handle non-finite values.
Results may differ from a plain program's by a relative error of at most 0.0001.
Values sent between devices are 32-bit elements; how exact they have to be, the bound alone decides.
A program may use at most 64 MiB of HBM per device.

v0:
```python
import jax
import jax.numpy as jnp
from jax import lax
from jax.sharding import PartitionSpec as P

time_step = 0.1
field_weight = 0.0625


def contract(form, first, second):
    return jnp.einsum(form, first, second, precision=lax.Precision.HIGHEST)


def right_product(stack, matrix):
    real = contract("mij,jk->mik", stack[:, 0], matrix[0]) - contract(
        "mij,jk->mik", stack[:, 1], matrix[1]
    )
    imag = contract("mij,jk->mik", stack[:, 0], matrix[1]) + contract(
        "mij,jk->mik", stack[:, 1], matrix[0]
    )
    return jnp.stack([real, imag], axis=1)


def advance(stack, commut, weights, dens):
    turned = jnp.stack([commut[:, 1], -commut[:, 0]], axis=1)
    return stack + time_step * turned + time_step * weights[:, None, None, None] * dens[None]


def gather_hamil(rows):
    return lax.all_gather(rows, "orb", axis=1, tiled=True)


def rows_substep(stacks, dens_rows, hamil, coupling):
    items, parts, row_count, width = stacks.shape
    blocks = lax.axis_size("orb")
    col_count = width // blocks
    right = right_product(stacks, hamil)
    outgoing = stacks.reshape(items, parts, row_count, blocks, col_count)
    outgoing = outgoing.transpose(0, 1, 3, 4, 2).reshape(
        items, parts, blocks, col_count * row_count
    )
    received = lax.all_to_all(outgoing, "orb", split_axis=2, concat_axis=2, tiled=True)
    count = received.shape[0]
    columns = received.reshape(count, parts, blocks, col_count, row_count)
    columns = columns.transpose(0, 1, 3, 2, 4).reshape(count, parts, col_count, width)
    real = contract("mcj,ij->mci", columns[:, 0], hamil[0]) - contract(
        "mcj,ij->mci", columns[:, 1], hamil[1]
    )
    imag = contract("mcj,ij->mci", columns[:, 0], hamil[1]) + contract(
        "mcj,ij->mci", columns[:, 1], hamil[0]
    )
    product = jnp.stack([real, imag], axis=1).reshape(count, parts, col_count, blocks, row_count)
    product = product.transpose(0, 1, 3, 2, 4).reshape(count, parts, blocks, col_count * row_count)
    returned = lax.all_to_all(product, "orb", split_axis=2, concat_axis=2, tiled=True)
    returned = returned.reshape(count, parts, blocks, col_count, row_count)
    left = returned.transpose(0, 1, 4, 2, 3).reshape(count, parts, row_count, width)
    updated = advance(stacks, left - right, coupling, dens_rows)
    partial_value = contract("m,mcrk->crk", coupling, updated)
    collision = lax.psum(partial_value, "mode")
    return (updated, dens_rows + time_step * collision)


def propagate(stacks, propagator):
    local_modes = stacks.shape[0]
    groups = lax.axis_size("mode")
    flat = stacks.reshape(local_modes, groups, -1)
    spread = lax.all_to_all(flat, "mode", split_axis=1, concat_axis=0, tiled=True)
    entries = spread[:, 0, :]
    mixed = contract("mn,nx->mx", lax.all_gather(propagator, "mode", axis=0, tiled=True), entries)
    returned = lax.all_to_all(mixed[:, None, :], "mode", split_axis=0, concat_axis=1, tiled=True)
    return returned.reshape(stacks.shape)


def on_device(correlators, density, bare_hamiltonian, coupling, propagator):
    dens_rows = density
    hamil = gather_hamil(bare_hamiltonian + field_weight * density)
    stacks = correlators
    for turn in range(2):
        stacks, dens_rows = rows_substep(stacks, dens_rows, hamil, coupling)
        hamil = gather_hamil(bare_hamiltonian + field_weight * dens_rows)
    stacks = propagate(stacks, propagator)
    stacks, dens_rows = rows_substep(stacks, dens_rows, hamil, coupling)
    return (stacks, dens_rows)


def solution(mesh):
    in_specs = (
        P("mode", None, "orb", None),
        P(None, "orb", None),
        P(None, "orb", None),
        P("mode"),
        P("mode", None),
    )
    out_specs = (P("mode", None, "orb", None), P(None, "orb", None))
    return jax.shard_map(
        on_device, mesh=mesh, in_specs=in_specs, out_specs=out_specs, check_vma=False
    )
```

profile of v0, /device:TPU:64, one launch (start us, length us, event | category | flops | bytes accessed | tf_op | source)
XLA Modules:
  0.0 806.2 jit_solution(5045939652481662568)
XLA Ops:
  15.4 10.0 %all-to-all-start = ((f32[16,2,16,256]{3,1,0,2:T(2,128)}), f32[16,2,16,256]{3,1,0,2:T(2,128)S(1)}, u32[]{:S(2)}, u32[]{:S(2)}) async-start(f32[16,2,16,256]{3,1,0,2:T(2,128)} %copy.38), calls=%async_computation | async-start | bytes 1048576 | tf_op jit(solution)/shard_map/all_to_all | solution.py:42
  25.4 25.8 %all_gather.12 = f32[2,256,256]{2,1,0:T(8,128)S(1)} all-gather(f32[2,16,256]{2,1,0:T(8,128)S(1)} %multiply_add_fusion.5), channel_id=1, replica_groups=mesh['mode'=32,'orb'=16] {'orb'}, dimensions={1}, use_global_device_ids=true | all-gather | bytes 557056 | tf_op jit(solution)/shard_map/all_gather | solution.py:30
  54.1 5.9 copy.40
  75.9 3.5 reshape.97
  80.6 7.9 all-to-all-start.1
  90.2 12.7 %all-to-all-done.1 = f32[16,2,16,256]{3,1,0,2:T(2,128)S(1)} async-done(((f32[16,2,16,256]{3,1,0,2:T(2,128)}), f32[16,2,16,256]{3,1,0,2:T(2,128)S(1)}, u32[]{:S(2)}, u32[]{:S(2)}) %all-to-all-start.1) | async-done | bytes 524320 | tf_op jit(solution)/shard_map/all_to_all | solution.py:54
  116.1 5.9 all-to-all-start.2
  122.7 143.3 %psum.21 = f32[2,16,256]{2,1,0:T(8,128)S(1)} all-reduce(f32[2,16,256]{2,1,0:T(8,128)S(1)} %bitcast.232), channel_id=1, replica_groups=mesh['mode'=32,'orb'=16] {'mode'}, use_global_device_ids=true, to_apply=%region_0.0 | all-reduce | flops 8192 | bytes 65536 | tf_op jit(solution)/shard_map/psum | solution.py:59
  266.0 17.0 %all_gather.13 = f32[2,256,256]{2,1,0:T(8,128)S(1)} all-gather(f32[2,16,256]{2,1,0:T(8,128)S(1)} %get-tuple-element.10), channel_id=1, replica_groups=mesh['mode'=32,'orb'=16] {'orb'}, dimensions={1}, use_global_device_ids=true | all-gather | bytes 557056 | tf_op jit(solution)/shard_map/all_gather | solution.py:30
  286.0 5.9 copy.52
  298.6 3.6 copy.53
  314.0 6.3 all-to-all-start.3
  323.3 11.4 %all-to-all-done.3 = f32[16,2,16,256]{3,1,0,2:T(2,128)S(1)} async-done(((f32[16,2,16,256]{3,1,0,2:T(2,128)}), f32[16,2,16,256]{3,1,0,2:T(2,128)S(1)}, u32[]{:S(2)}, u32[]{:S(2)}) %all-to-all-start.3) | async-done | bytes 524320 | tf_op jit(solution)/shard_map/all_to_all | solution.py:54
  341.9 3.9 all-to-all-start.4
  345.8 54.7 %all-gather.2.cloned.1.call-done = f32[512,512]{1,0:T(8,128)} async-done(((f32[16,512]{1,0:T(8,128)}), f32[512,512]{1,0:T(8,128)}) %all-gather.2.cloned.1.call-update) | async-done | bytes 1048592 | tf_op jit(solution)/shard_map/all_gather | solution.py:69
  404.0 19.9 %all_to_all.60 = f32[512,1,256]{2,1,0:T(1,128)S(1)} all-to-all(f32[512,1,256]{2,1,0:T(1,128)S(1)} %copy.60), channel_id=1, replica_groups=mesh['mode'=32,'orb'=16] {'mode'}, dimensions={0} | all-to-all | bytes 1048576 | tf_op jit(solution)/shard_map/all_to_all | solution.py:70
  426.5 5.9 copy.62
  437.1 7.8 all-to-all-start.6
  445.5 139.6 %psum.22 = f32[2,16,256]{2,1,0:T(8,128)S(1)} all-reduce(f32[2,16,256]{2,1,0:T(8,128)S(1)} %bitcast.233), channel_id=1, replica_groups=mesh['mode'=32,'orb'=16] {'mode'}, use_global_device_ids=true, to_apply=%region_1.0 | all-reduce | flops 8192 | bytes 65536 | tf_op jit(solution)/shard_map/psum | solution.py:59
  585.2 17.2 %all_gather.15 = f32[2,256,256]{2,1,0:T(8,128)S(1)} all-gather(f32[2,16,256]{2,1,0:T(8,128)S(1)} %get-tuple-element.8), channel_id=1, replica_groups=mesh['mode'=32,'orb'=16] {'orb'}, dimensions={1}, use_global_device_ids=true | all-gather | bytes 557056 | tf_op jit(solution)/shard_map/all_gather | solution.py:30
  605.4 5.9 copy.65
  631.8 6.7 all-to-all-start.7
  640.4 12.5 %all-to-all-done.7 = f32[16,2,16,256]{3,1,0,2:T(2,128)S(1)} async-done(((f32[16,2,16,256]{3,1,0,2:T(2,128)}), f32[16,2,16,256]{3,1,0,2:T(2,128)S(1)}, u32[]{:S(2)}, u32[]{:S(2)}) %all-to-all-start.7) | async-done | bytes 524320 | tf_op jit(solution)/shard_map/all_to_all | solution.py:54
  660.6 137.7 %psum.23 = f32[2,16,256]{2,1,0:T(8,128)S(1)} all-reduce(f32[2,16,256]{2,1,0:T(8,128)S(1)} %bitcast.234), channel_id=1, replica_groups=mesh['mode'=32,'orb'=16] {'mode'}, use_global_device_ids=true, to_apply=%region_2.0 | all-reduce | flops 8192 | bytes 65536 | tf_op jit(solution)/shard_map/psum | solution.py:59
  (123 shorter events, 120.2 us)
Async XLA Ops:
  10.7 14.7 %copy-start.7 = (f32[2,16,256]{2,1,0:T(8,128)S(1)}, f32[2,16,256]{2,1,0:T(8,128)}, u32[]{:S(2)}) copy-start(f32[2,16,256]{2,1,0:T(8,128)} %param.6) | copy-start | bytes 98308
  10.7 14.7 %copy-start.8 = (f32[2,16,256]{2,1,0:T(8,128)S(1)}, f32[2,16,256]{2,1,0:T(8,128)}, u32[]{:S(2)}) copy-start(f32[2,16,256]{2,1,0:T(8,128)} %param.7) | copy-start | bytes 98308
  15.4 35.8 %all-to-all-start = ((f32[16,2,16,256]{3,1,0,2:T(2,128)}), f32[16,2,16,256]{3,1,0,2:T(2,128)S(1)}, u32[]{:S(2)}, u32[]{:S(2)}) async-start(f32[16,2,16,256]{3,1,0,2:T(2,128)} %copy.38), calls=%async_computation | async-start | bytes 1048576 | tf_op jit(solution)/shard_map/all_to_all | solution.py:42
  72.0 1.6 copy-start.1
  75.9 12.7 %copy-start = (f32[16,2,16,256]{3,2,1,0:T(8,128)S(1)}, f32[16,2,16,256]{3,2,1,0:T(8,128)}, u32[]{:S(2)}) copy-start(f32[16,2,16,256]{3,2,1,0:T(8,128)} %param.5) | copy-start | bytes 1572868
  79.4 10.7 %copy-start.9 = (f32[16]{0:T(128)S(1)}, f32[16]{0:T(128)}, u32[]{:S(2)}) copy-start(f32[16]{0:T(128)} %param.8) | copy-start | bytes 196
  80.6 22.2 %all-to-all-start.1 = ((f32[16,2,16,256]{3,1,0,2:T(2,128)}), f32[16,2,16,256]{3,1,0,2:T(2,128)S(1)}, u32[]{:S(2)}, u32[]{:S(2)}) async-start(f32[16,2,16,256]{3,1,0,2:T(2,128)} %copy.43), calls=%async_computation.1 | async-start | bytes 1048576 | tf_op jit(solution)/shard_map/all_to_all | solution.py:54
  116.1 166.9 %all-to-all-start.2 = ((f32[16,2,16,256]{3,1,0,2:T(2,128)}), f32[16,2,16,256]{3,1,0,2:T(2,128)S(1)}, u32[]{:S(2)}, u32[]{:S(2)}) async-start(f32[16,2,16,256]{3,1,0,2:T(2,128)} %copy.50), calls=%async_computation.2 | async-start | bytes 1048576 | tf_op jit(solution)/shard_map/all_to_all | solution.py:42
  304.6 2.4 copy-start.2
  314.0 20.7 %all-to-all-start.3 = ((f32[16,2,16,256]{3,1,0,2:T(2,128)}), f32[16,2,16,256]{3,1,0,2:T(2,128)S(1)}, u32[]{:S(2)}, u32[]{:S(2)}) async-start(f32[16,2,16,256]{3,1,0,2:T(2,128)} %copy.55), calls=%async_computation.3 | async-start | bytes 1048576 | tf_op jit(solution)/shard_map/all_to_all | solution.py:54
  320.3 80.1 %all-gather.2.cloned.1.call-start = ((), (), s32[]{:S(2)}) async-start(), calls=%async_computation.8 | async-start | bytes 1081344 | tf_op jit(solution)/shard_map/all_gather | solution.py:69
  335.0 5.4 copy-start.6
  341.9 58.6 %all-to-all-start.4 = ((f32[16,32,256]{2,0,1:T(8,128)}), f32[16,32,256]{2,0,1:T(8,128)S(1)}, u32[]{:S(2)}, u32[]{:S(2)}) async-start(f32[16,32,256]{2,0,1:T(8,128)} %copy.59), calls=%async_computation.4 | async-start | bytes 1048576 | tf_op jit(solution)/shard_map/all_to_all | solution.py:67
  437.1 165.4 %all-to-all-start.6 = ((f32[16,2,16,256]{3,1,0,2:T(2,128)}), f32[16,2,16,256]{3,1,0,2:T(2,128)S(1)}, u32[]{:S(2)}, u32[]{:S(2)}) async-start(f32[16,2,16,256]{3,1,0,2:T(2,128)} %copy.63), calls=%async_computation.6 | async-start | bytes 1048576 | tf_op jit(solution)/shard_map/all_to_all | solution.py:42
  614.8 0.9 copy-start.4
  618.4 2.0 copy-start.5
  623.2 1.6 copy-start.3
  631.8 21.0 %all-to-all-start.7 = ((f32[16,2,16,256]{3,1,0,2:T(2,128)}), f32[16,2,16,256]{3,1,0,2:T(2,128)S(1)}, u32[]{:S(2)}, u32[]{:S(2)}) async-start(f32[16,2,16,256]{3,1,0,2:T(2,128)} %copy.68), calls=%async_computation.7 | async-start | bytes 1048576 | tf_op jit(solution)/shard_map/all_to_all | solution.py:54
Sparse Core Ops, SparseCore 0:
  324.3 76.0 all-gather.1
where the time goes:
time: 816 us; the launch traced here: 806 us
  blocking collectives  501 us (61%)
  local copies, waits for them, and re-layouts  123 us (15%)
  waiting for transfers between devices  91.7 us (11%)
  starting transfers between devices  48.6 us (6%)
  matrix products  18.3 us (2%)
  between operations  15.1 us (2%)
  other arithmetic  8.6 us (1%)
    psum x3, blocking collectives, rows_substep(): collision = lax.psum(partial_value, 'mode')  421 us
    all_gather x3, blocking collectives, gather_hamil(): return lax.all_gather(rows, 'orb', axis=1, tiled=True)  60.1 us
    all_gather x1, waiting for transfers between devices, propagate(): lax.all_gather(propagator, 'mode', axis=0, tiled=True)  54.7 us
    all_to_all x3, waiting for transfers between devices, rows_substep(): lax.all_to_all(product, 'orb', split_axis=2, concat_axis=2, tiled=True)  36.5 us
    all_to_all x3, starting transfers between devices, rows_substep(): lax.all_to_all(outgoing, 'orb', split_axis=2, concat_axis=2, tiled=True)  23.6 us
    another operation x12, local copies, waits for them, and re-layouts, rows_substep(): jnp.stack([real, imag], axis=1)  21.9 us
    all_to_all x3, starting transfers between devices, rows_substep(): lax.all_to_all(product, 'orb', split_axis=2, concat_axis=2, tiled=True)  20.9 us
    all_to_all x1, blocking collectives, propagate(): lax.all_to_all(mixed[:, None, :], 'mode', split_axis=0, concat_axis=1, ti...  19.9 us
  transfers between devices with their start and end apart: 8, of which 4 were waited for; matrix products, arithmetic and copies ran while one was open for 2% of the time, Pallas kernels for 0%

commit v1 on v0

--- a/solution.py
+++ b/solution.py
@@ -56,7 +56,7 @@
     left = returned.transpose(0, 1, 4, 2, 3).reshape(count, parts, row_count, width)
     updated = advance(stacks, left - right, coupling, dens_rows)
     partial_value = contract("m,mcrk->crk", coupling, updated)
-    collision = lax.psum(partial_value, "mode")
+    collision = jnp.sum(lax.all_gather(partial_value, "mode"), axis=0)
     return (updated, dens_rows + time_step * collision)
 
 

time: 816 us -> 577 us (0.71)
  the two profiles are of different devices: /device:TPU:64 before, /device:TPU:16 now
where the time goes in v1:
time: 577 us; the launch traced here: 567 us
  waiting for transfers between devices  252 us (44%)
  local copies, waits for them, and re-layouts  125 us (22%)
  blocking collectives  105 us (18%)
  starting transfers between devices  39.7 us (7%)
  matrix products  18.3 us (3%)
  between operations  14.6 us (3%)
  other arithmetic  12.6 us (2%)
    all_gather x3, waiting for transfers between devices, rows_substep(): collision = jnp.sum(lax.all_gather(partial_value, 'mode'), axis=0)  157 us
    all_gather x3, blocking collectives, gather_hamil(): return lax.all_gather(rows, 'orb', axis=1, tiled=True)  67.1 us
    all_gather x1, waiting for transfers between devices, propagate(): lax.all_gather(propagator, 'mode', axis=0, tiled=True)  52.8 us
    all_to_all x3, waiting for transfers between devices, rows_substep(): lax.all_to_all(product, 'orb', split_axis=2, concat_axis=2, tiled=True)  41.3 us
    another operation x12, local copies, waits for them, and re-layouts, rows_substep(): jnp.stack([real, imag], axis=1)  21.9 us
    all_to_all x1, blocking collectives, rows_substep(): lax.all_to_all(outgoing, 'orb', split_axis=2, concat_axis=2, tiled=True)  20 us
    dot_general x28, matrix products, contract(): return jnp.einsum(form, first, second, precision=lax.Precision.HIGHEST)  18.3 us
    all_to_all x1, blocking collectives, propagate(): lax.all_to_all(mixed[:, None, :], 'mode', split_axis=0, concat_axis=1, ti...  18.2 us
  transfers between devices with their start and end apart: 10, of which 7 were waited for; matrix products, arithmetic and copies ran while one was open for 9% of the time, Pallas kernels for 0%

profile of v1, /device:TPU:16, one launch (start us, length us, event | category | flops | bytes accessed | tf_op | source)
XLA Modules:
  0.0 567.0 jit_solution(2373474604854496438)
XLA Ops:
  15.4 10.4 %all-to-all-start = ((f32[16,2,16,256]{3,1,0,2:T(2,128)}), f32[16,2,16,256]{3,1,0,2:T(2,128)S(1)}, u32[]{:S(2)}, u32[]{:S(2)}) async-start(f32[16,2,16,256]{3,1,0,2:T(2,128)} %copy.38), calls=%async_computation | async-start | bytes 1048576 | tf_op jit(solution)/shard_map/all_to_all | solution.py:42
  25.9 27.4 %all_gather.30 = f32[2,256,256]{2,1,0:T(8,128)S(1)} all-gather(f32[2,16,256]{2,1,0:T(8,128)S(1)} %multiply_add_fusion.5), channel_id=1, replica_groups=mesh['mode'=32,'orb'=16] {'orb'}, dimensions={1}, use_global_device_ids=true | all-gather | bytes 557056 | tf_op jit(solution)/shard_map/all_gather | solution.py:30
  56.2 5.9 %copy.40 = f32[16,2,16,16,16]{4,3,2,0,1:T(8,128)} copy(f32[16,2,16,16,16]{4,2,3,1,0:T(8,128)} %bitcast.226) | data formatting | bytes 1048576 | tf_op jit(solution)/shard_map/transpose | solution.py:45
  78.0 3.5 reshape.97
  82.7 6.1 %all-to-all-start.1 = ((f32[16,2,16,256]{3,1,0,2:T(2,128)}), f32[16,2,16,256]{3,1,0,2:T(2,128)S(1)}, u32[]{:S(2)}, u32[]{:S(2)}) async-start(f32[16,2,16,256]{3,1,0,2:T(2,128)} %copy.43), calls=%async_computation.1 | async-start | bytes 1048576 | tf_op jit(solution)/shard_map/all_to_all | solution.py:54
  90.6 14.3 %all-to-all-done.1 = f32[16,2,16,256]{3,1,0,2:T(2,128)S(1)} async-done(((f32[16,2,16,256]{3,1,0,2:T(2,128)}), f32[16,2,16,256]{3,1,0,2:T(2,128)S(1)}, u32[]{:S(2)}, u32[]{:S(2)}) %all-to-all-start.1) | async-done | bytes 524320 | tf_op jit(solution)/shard_map/all_to_all | solution.py:54
  118.8 20.0 %all_to_all.60 = f32[16,2,16,256]{3,1,0,2:T(2,128)S(1)} all-to-all(f32[16,2,16,256]{3,1,0,2:T(2,128)S(1)} %copy.50), channel_id=1, replica_groups=mesh['mode'=32,'orb'=16] {'orb'}, dimensions={2} | all-to-all | bytes 1048576 | tf_op jit(solution)/shard_map/all_to_all | solution.py:42
  141.7 5.9 %copy.52 = f32[16,2,16,16,16]{4,3,2,0,1:T(8,128)} copy(f32[16,2,16,16,16]{4,2,3,1,0:T(8,128)} %bitcast.227) | data formatting | bytes 1048576 | tf_op jit(solution)/shard_map/transpose | solution.py:45
  151.2 40.9 %all-gather.10.cloned.1.call-done = f32[64,16,256]{2,1,0:T(8,128)} async-done(((f32[2,16,256]{2,1,0:T(8,128)}), f32[64,16,256]{2,1,0:T(8,128)}) %all-gather.10.cloned.1.call-update) | async-done | bytes 1048592 | tf_op jit(solution)/shard_map/all_gather | solution.py:59
  193.3 19.7 %all_gather.33 = f32[2,256,256]{2,1,0:T(8,128)S(1)} all-gather(f32[2,16,256]{2,1,0:T(8,128)S(1)} %get-tuple-element.10), channel_id=1, replica_groups=mesh['mode'=32,'orb'=16] {'orb'}, dimensions={1}, use_global_device_ids=true | all-gather | bytes 557056 | tf_op jit(solution)/shard_map/all_gather | solution.py:30
  216.3 3.6 copy.53
  231.7 4.3 all-to-all-start.3
  239.0 13.0 %all-to-all-done.3 = f32[16,2,16,256]{3,1,0,2:T(2,128)S(1)} async-done(((f32[16,2,16,256]{3,1,0,2:T(2,128)}), f32[16,2,16,256]{3,1,0,2:T(2,128)S(1)}, u32[]{:S(2)}, u32[]{:S(2)}) %all-to-all-start.3) | async-done | bytes 524320 | tf_op jit(solution)/shard_map/all_to_all | solution.py:54
  259.2 6.5 %all-to-all-start.4 = ((f32[16,32,256]{2,0,1:T(8,128)}), f32[16,32,256]{2,0,1:T(8,128)S(1)}, u32[]{:S(2)}, u32[]{:S(2)}) async-start(f32[16,32,256]{2,0,1:T(8,128)} %copy.59), calls=%async_computation.4 | async-start | bytes 1048576 | tf_op jit(solution)/shard_map/all_to_all | solution.py:67
  267.4 52.8 %all-gather.8.cloned.1.call-done = f32[512,512]{1,0:T(8,128)} async-done(((f32[16,512]{1,0:T(8,128)}), f32[512,512]{1,0:T(8,128)}) %all-gather.8.cloned.1.call-update) | async-done | bytes 1048592 | tf_op jit(solution)/shard_map/all_gather | solution.py:69
  323.7 18.2 %all_to_all.61 = f32[512,1,256]{2,1,0:T(1,128)S(1)} all-to-all(f32[512,1,256]{2,1,0:T(1,128)S(1)} %copy.60), channel_id=1, replica_groups=mesh['mode'=32,'orb'=16] {'mode'}, dimensions={0} | all-to-all | bytes 1048576 | tf_op jit(solution)/shard_map/all_to_all | solution.py:70
  344.6 5.9 %copy.62 = f32[16,2,16,16,16]{2,4,3,1,0:T(8,128)} copy(f32[16,2,16,16,16]{4,3,0,2,1:T(8,128)} %reshape_reshape.3) | data formatting | bytes 1048576 | tf_op jit(solution)/shard_map/reshape;reshape | solution.py:38
  355.2 7.5 %all-to-all-start.6 = ((f32[16,2,16,256]{3,1,0,2:T(2,128)}), f32[16,2,16,256]{3,1,0,2:T(2,128)S(1)}, u32[]{:S(2)}, u32[]{:S(2)}) async-start(f32[16,2,16,256]{3,1,0,2:T(2,128)} %copy.63), calls=%async_computation.6 | async-start | bytes 1048576 | tf_op jit(solution)/shard_map/all_to_all | solution.py:42
  362.7 40.7 %all-gather.12.cloned.1.call-done = f32[64,16,256]{2,1,0:T(8,128)} async-done(((f32[2,16,256]{2,1,0:T(8,128)}), f32[64,16,256]{2,1,0:T(8,128)}) %all-gather.12.cloned.1.call-update) | async-done | bytes 1048592 | tf_op jit(solution)/shard_map/all_gather | solution.py:59
  404.7 20.0 %all_gather.37 = f32[2,256,256]{2,1,0:T(8,128)S(1)} all-gather(f32[2,16,256]{2,1,0:T(8,128)S(1)} %get-tuple-element.8), channel_id=1, replica_groups=mesh['mode'=32,'orb'=16] {'orb'}, dimensions={1}, use_global_device_ids=true | all-gather | bytes 557056 | tf_op jit(solution)/shard_map/all_gather | solution.py:30
  427.6 5.9 %copy.65 = f32[16,2,16,16,16]{4,3,2,0,1:T(8,128)} copy(f32[16,2,16,16,16]{4,2,3,1,0:T(8,128)} %bitcast.229) | data formatting | bytes 1048576 | tf_op jit(solution)/shard_map/transpose | solution.py:45
  454.2 4.3 all-to-all-start.7
  460.5 13.9 %all-to-all-done.7 = f32[16,2,16,256]{3,1,0,2:T(2,128)S(1)} async-done(((f32[16,2,16,256]{3,1,0,2:T(2,128)}), f32[16,2,16,256]{3,1,0,2:T(2,128)S(1)}, u32[]{:S(2)}, u32[]{:S(2)}) %all-to-all-start.7) | async-done | bytes 524320 | tf_op jit(solution)/shard_map/all_to_all | solution.py:54
  482.9 75.4 %all-gather.14.cloned.1.call-done = f32[64,16,256]{2,1,0:T(8,128)} async-done(((f32[2,16,256]{2,1,0:T(8,128)}), f32[64,16,256]{2,1,0:T(8,128)}) %all-gather.14.cloned.1.call-update) | async-done | bytes 1048592 | tf_op jit(solution)/shard_map/all_gather | solution.py:59
  (131 shorter events, 126.0 us)
Async XLA Ops:
  10.7 15.1 %copy-start.7 = (f32[2,16,256]{2,1,0:T(8,128)S(1)}, f32[2,16,256]{2,1,0:T(8,128)}, u32[]{:S(2)}) copy-start(f32[2,16,256]{2,1,0:T(8,128)} %param.6) | copy-start | bytes 98308
  10.7 15.1 %copy-start.8 = (f32[2,16,256]{2,1,0:T(8,128)S(1)}, f32[2,16,256]{2,1,0:T(8,128)}, u32[]{:S(2)}) copy-start(f32[2,16,256]{2,1,0:T(8,128)} %param.7) | copy-start | bytes 98308
  15.4 37.8 %all-to-all-start = ((f32[16,2,16,256]{3,1,0,2:T(2,128)}), f32[16,2,16,256]{3,1,0,2:T(2,128)S(1)}, u32[]{:S(2)}, u32[]{:S(2)}) async-start(f32[16,2,16,256]{3,1,0,2:T(2,128)} %copy.38), calls=%async_computation | async-start | bytes 1048576 | tf_op jit(solution)/shard_map/all_to_all | solution.py:42
  74.0 1.6 copy-start.1
  78.0 11.0 %copy-start = (f32[16,2,16,256]{3,2,1,0:T(8,128)S(1)}, f32[16,2,16,256]{3,2,1,0:T(8,128)}, u32[]{:S(2)}) copy-start(f32[16,2,16,256]{3,2,1,0:T(8,128)} %param.5) | copy-start | bytes 1572868
  81.5 9.0 %copy-start.9 = (f32[16]{0:T(128)S(1)}, f32[16]{0:T(128)}, u32[]{:S(2)}) copy-start(f32[16]{0:T(128)} %param.8) | copy-start | bytes 196
  82.7 22.2 %all-to-all-start.1 = ((f32[16,2,16,256]{3,1,0,2:T(2,128)}), f32[16,2,16,256]{3,1,0,2:T(2,128)S(1)}, u32[]{:S(2)}, u32[]{:S(2)}) async-start(f32[16,2,16,256]{3,1,0,2:T(2,128)} %copy.43), calls=%async_computation.1 | async-start | bytes 1048576 | tf_op jit(solution)/shard_map/all_to_all | solution.py:54
  88.9 103.1 %all-gather.10.cloned.1.call-start = ((), (), s32[]{:S(2)}) async-start(), calls=%async_computation.9 | async-start | bytes 1081344 | tf_op jit(solution)/shard_map/all_gather | solution.py:59
  222.3 2.4 copy-start.2
  231.7 20.3 %all-to-all-start.3 = ((f32[16,2,16,256]{3,1,0,2:T(2,128)}), f32[16,2,16,256]{3,1,0,2:T(2,128)S(1)}, u32[]{:S(2)}, u32[]{:S(2)}) async-start(f32[16,2,16,256]{3,1,0,2:T(2,128)} %copy.55), calls=%async_computation.3 | async-start | bytes 1048576 | tf_op jit(solution)/shard_map/all_to_all | solution.py:54
  236.0 84.2 %all-gather.8.cloned.1.call-start = ((), (), s32[]{:S(2)}) async-start(), calls=%async_computation.8 | async-start | bytes 1081344 | tf_op jit(solution)/shard_map/all_gather | solution.py:69
  252.3 5.4 copy-start.6
  259.2 61.0 %all-to-all-start.4 = ((f32[16,32,256]{2,0,1:T(8,128)}), f32[16,32,256]{2,0,1:T(8,128)S(1)}, u32[]{:S(2)}, u32[]{:S(2)}) async-start(f32[16,32,256]{2,0,1:T(8,128)} %copy.59), calls=%async_computation.4 | async-start | bytes 1048576 | tf_op jit(solution)/shard_map/all_to_all | solution.py:67
  265.8 137.6 %all-gather.12.cloned.1.call-start = ((), (), s32[]{:S(2)}) async-start(), calls=%async_computation.10 | async-start | bytes 1081344 | tf_op jit(solution)/shard_map/all_gather | solution.py:59
  355.2 69.5 %all-to-all-start.6 = ((f32[16,2,16,256]{3,1,0,2:T(2,128)}), f32[16,2,16,256]{3,1,0,2:T(2,128)S(1)}, u32[]{:S(2)}, u32[]{:S(2)}) async-start(f32[16,2,16,256]{3,1,0,2:T(2,128)} %copy.63), calls=%async_computation.6 | async-start | bytes 1048576 | tf_op jit(solution)/shard_map/all_to_all | solution.py:42
  437.1 0.9 copy-start.4
  440.7 2.0 copy-start.5
  445.6 1.6 copy-start.3
  454.2 20.3 %all-to-all-start.7 = ((f32[16,2,16,256]{3,1,0,2:T(2,128)}), f32[16,2,16,256]{3,1,0,2:T(2,128)S(1)}, u32[]{:S(2)}, u32[]{:S(2)}) async-start(f32[16,2,16,256]{3,1,0,2:T(2,128)} %copy.68), calls=%async_computation.7 | async-start | bytes 1048576 | tf_op jit(solution)/shard_map/all_to_all | solution.py:54
  458.5 99.9 %all-gather.14.cloned.1.call-start = ((), (), s32[]{:S(2)}) async-start(), calls=%async_computation.11 | async-start | bytes 1081344 | tf_op jit(solution)/shard_map/all_gather | solution.py:59
Sparse Core Ops, SparseCore 0:
  112.4 79.6 all-gather.9
  240.0 80.1 all-gather.7
  324.0 79.3 all-gather.11
  482.2 76.0 all-gather.13
